TPU v7x, 512 devices: a whole 4x4x16 slice. The times are simulated.
512 devices in a mesh: lat: 16 (over x_hi, y, core), lon: 32 (over z, x_lo).
Axes of the slice: x: 4 (x_hi: 2, x_lo: 2; x = x_hi * 2 + x_lo), y: 4, z: 16, core: 2. Of those that a mesh axis runs over, the one named last changes fastest.
Arguments:
- tokens: bfloat16 [2, 192, 384, 1024], P(None, 'lat', 'lon'), may hold values from -96 to 96
- qkv_weight: bfloat16 [1024, 1536], P('lon'), may hold values from -0.1875 to 0.1875
- out_weight: bfloat16 [512, 1024], P('lon'), may hold values from -1 to 1
- norm_gain: float32 [1024], replicated, may hold values from 0.1 to 1.9
- norm_bias: float32 [1024], replicated, may hold values from -3 to 3
- mixed_grad: bfloat16 [2, 192, 384, 1024], P(None, 'lat', 'lon'), may hold values from -6 to 6
Outputs:
- mixed: bfloat16 [2, 192, 384, 1024], P(None, 'lat', 'lon')
- token_grad: bfloat16 [2, 192, 384, 1024], P(None, 'lat', 'lon')
All inputs are finite; a program needn't handle non-finite values.
Results may differ from a plain program's by a relative error of at most 0.014.
The roundings to bfloat16 on the way count: a program that leaves them out, or rounds other values in their place, can miss the bound.
Values may be sent and summed in bfloat16 or wider, within the bound.
A program may use at most 64 MiB of HBM per device.

v0:
```python
import jax
import jax.numpy as jnp
from jax import lax
from jax.sharding import PartitionSpec as P

HEADS = 8
HEAD_DIM = 64
LEV = 2
WIN = 12
INNER = 512
HALF = 6


norm_eps = 1e-05


def from_behind(shard, axis, by):
    size = lax.axis_size(axis)
    return lax.ppermute(shard, axis, [(i, (i + by) % size) for i in range(size)])


def to_shifted(grid_field):
    lon_strip = from_behind(grid_field[:, :, :HALF], "lon", -1)
    widened = jnp.concatenate([grid_field[:, :, HALF:], lon_strip], axis=2)
    lat_strip = from_behind(widened[:, :HALF], "lat", -1)
    return jnp.concatenate([widened[:, HALF:], lat_strip], axis=1)


def to_grid(moved_field):
    lat_count = moved_field.shape[1]
    lat_strip = from_behind(moved_field[:, lat_count - HALF :], "lat", 1)
    lowered = jnp.concatenate([lat_strip, moved_field[:, : lat_count - HALF]], axis=1)
    lon_count = lowered.shape[2]
    lon_strip = from_behind(lowered[:, :, lon_count - HALF :], "lon", 1)
    return jnp.concatenate([lon_strip, lowered[:, :, : lon_count - HALF]], axis=2)


def to_windows(grid_field):
    levels, lat_count, lon_count, feature = grid_field.shape
    blocks = grid_field.reshape(levels, lat_count, lon_count // WIN, WIN, feature).transpose(
        2, 0, 1, 3, 4
    )
    return blocks.reshape(lon_count // WIN, levels * lat_count * WIN, feature)


def from_windows(blocks):
    window_count, window_size, feature = blocks.shape
    grid_field = blocks.reshape(window_count, LEV, WIN, WIN, feature).transpose(1, 2, 0, 3, 4)
    return grid_field.reshape(LEV, WIN, window_count * WIN, feature)


def times_transposed(left, right):
    return lax.dot_general(
        left, right, (((1,), (1,)), ((), ())), preferred_element_type=jnp.float32
    )


def per_device(tokens, qkv_weight, out_weight, norm_gain, norm_bias, mixed_grad):
    levels, lat_count, lon_count, width = tokens.shape
    window_count = lon_count // WIN
    window_size = LEV * WIN * WIN
    factor = HEAD_DIM ** (-0.5)
    lat_rows = lax.axis_index("lat") * WIN + jnp.arange(WIN, dtype=jnp.int32)
    wrapped = lat_rows >= WIN * lax.axis_size("lat") - HALF
    wrapped = jnp.broadcast_to(wrapped[None, :, None], (LEV, WIN, WIN)).reshape(window_size)
    same_side = wrapped[:, None] == wrapped[None, :]
    whole_qkv, whole_out = (
        lax.all_gather(qkv_weight, "lon", axis=0, tiled=True),
        lax.all_gather(out_weight, "lon", axis=0, tiled=True),
    )
    shifted = to_windows(to_shifted(tokens))
    packed = jnp.dot(
        shifted.reshape(-1, width), whole_qkv, preferred_element_type=jnp.float32
    ).astype(jnp.bfloat16)
    packed = packed.reshape(window_count, window_size, 3, HEADS, HEAD_DIM)
    query_heads = packed[:, :, 0]
    key_heads = packed[:, :, 1]
    value_heads = packed[:, :, 2]
    scores = (
        jnp.einsum("wqhe,wkhe->whqk", query_heads, key_heads, preferred_element_type=jnp.float32)
        * factor
    )
    scores = jnp.where(same_side, scores, -jnp.inf)
    highest = jnp.max(scores, axis=-1, keepdims=True)
    raised = jnp.exp(scores - highest)
    probs = (raised / jnp.sum(raised, axis=-1, keepdims=True)).astype(jnp.bfloat16)
    heads = jnp.einsum(
        "whqk,wkhe->wqhe", probs, value_heads, preferred_element_type=jnp.float32
    ).astype(jnp.bfloat16)
    heads = heads.reshape(window_count, window_size, INNER)
    attn_moved = jnp.dot(
        heads.reshape(-1, INNER), whole_out, preferred_element_type=jnp.float32
    ).astype(jnp.bfloat16)
    attn = to_grid(from_windows(attn_moved.reshape(window_count, window_size, width)))
    attn_f = attn.astype(jnp.float32)
    centered = attn_f - jnp.mean(attn_f, axis=-1, keepdims=True)
    inverse = lax.rsqrt(jnp.mean(centered * centered, axis=-1, keepdims=True) + norm_eps)
    normed = centered * inverse
    mixed = (tokens.astype(jnp.float32) + normed * norm_gain + norm_bias).astype(jnp.bfloat16)
    scaled = mixed_grad.astype(jnp.float32) * norm_gain
    attn_grad = (
        scaled
        - jnp.mean(scaled, axis=-1, keepdims=True)
        - normed * jnp.mean(scaled * normed, axis=-1, keepdims=True)
    ) * inverse
    attn_grad = attn_grad.astype(jnp.bfloat16)
    grad_moved = to_windows(to_shifted(attn_grad))
    heads_grad = times_transposed(grad_moved.reshape(-1, width), whole_out).astype(jnp.bfloat16)
    heads_grad = heads_grad.reshape(window_count, window_size, HEADS, HEAD_DIM)
    prob_grad = jnp.einsum(
        "wqhe,wkhe->whqk", heads_grad, value_heads, preferred_element_type=jnp.float32
    )
    value_grad = jnp.einsum(
        "whqk,wqhe->wkhe", probs, heads_grad, preferred_element_type=jnp.float32
    ).astype(jnp.bfloat16)
    probs_f = probs.astype(jnp.float32)
    score_grad = (
        probs_f * (prob_grad - jnp.sum(probs_f * prob_grad, axis=-1, keepdims=True)) * factor
    )
    score_grad = score_grad.astype(jnp.bfloat16)
    query_grad = jnp.einsum(
        "whqk,wkhe->wqhe", score_grad, key_heads, preferred_element_type=jnp.float32
    ).astype(jnp.bfloat16)
    key_grad = jnp.einsum(
        "whqk,wqhe->wkhe", score_grad, query_heads, preferred_element_type=jnp.float32
    ).astype(jnp.bfloat16)
    packed_grad = jnp.stack([query_grad, key_grad, value_grad], axis=2).reshape(-1, 3 * INNER)
    shifted_grad = times_transposed(packed_grad, whole_qkv).astype(jnp.bfloat16)
    shifted_grad = shifted_grad.reshape(window_count, window_size, width)
    returned = to_grid(from_windows(shifted_grad))
    token_grad = (mixed_grad.astype(jnp.float32) + returned.astype(jnp.float32)).astype(
        jnp.bfloat16
    )
    return (mixed, token_grad)


def solution(mesh):
    placed = (
        P(None, "lat", "lon", None),
        P("lon", None),
        P("lon", None),
        P(),
        P(),
        P(None, "lat", "lon", None),
    )
    return jax.shard_map(
        per_device,
        mesh=mesh,
        in_specs=placed,
        out_specs=(P(None, "lat", "lon", None), P(None, "lat", "lon", None)),
        check_vma=False,
    )
```

profile of v0, /device:TPU:4, one launch (start us, length us, event | category | flops | bytes accessed | tf_op | source)
XLA Modules:
  0.0 397.1 jit_solution(17605931803635830257)
XLA Ops:
  9.4 12.0 %collective-permute-start = (bf16[2,12,6,1024]{3,0,2,1:T(2,128)(2,1)S(1)}, bf16[2,12,6,1024]{3,0,2,1:T(2,128)(2,1)S(1)}, u32[]{:S(2)}, u32[]{:S(2)}) collective-permute-start(bf16[2,12,6,1024]{3,0,2,1:T(2,128)(2,1)S(1)} %get-tuple-element.21), channel_id=1, source_target_pairs={{0,31},{1,0},{2,1},{3,2},{4,3},{5,4},{6,5},{7,6},{8,7},{9,8},{10,9... | collective-permute-start | bytes 884744 | tf_op jit(solution)/shard_map/ppermute | solution.py:19
  21.5 6.2 %collective-permute-done = bf16[2,12,6,1024]{3,0,2,1:T(2,128)(2,1)S(1)} collective-permute-done((bf16[2,12,6,1024]{3,0,2,1:T(2,128)(2,1)S(1)}, bf16[2,12,6,1024]{3,0,2,1:T(2,128)(2,1)S(1)}, u32[]{:S(2)}, u32[]{:S(2)}) %collective-permute-start) | collective-permute-done | bytes 294944 | tf_op jit(solution)/shard_map/ppermute | solution.py:19
  28.5 3.7 collective-permute-start.1
  32.5 5.7 %collective-permute-done.1 = bf16[2,6,12,1024]{3,0,2,1:T(2,128)(2,1)S(1)} collective-permute-done((bf16[2,6,12,1024]{3,0,2,1:T(2,128)(2,1)S(1)}, bf16[2,6,12,1024]{3,0,2,1:T(2,128)(2,1)S(1)}, u32[]{:S(2)}, u32[]{:S(2)}) %collective-permute-start.1) | collective-permute-done | bytes 294944 | tf_op jit(solution)/shard_map/ppermute | solution.py:19
  39.3 112.8 %all-gather.3.cloned.1.call-done = bf16[1024,1536]{1,0:T(8,128)(2,1)} async-done(((bf16[32,1536]{1,0:T(8,128)(2,1)}), bf16[1024,1536]{1,0:T(8,128)(2,1)}) %all-gather.3.cloned.1.call-update) | async-done | bytes 3145744 | tf_op jit(solution)/shard_map/all_gather | solution.py:68
  152.2 3.0 convolution_convert_fusion
  159.3 122.9 %all-gather.5.cloned.1.call-done = bf16[512,1024]{1,0:T(8,128)(2,1)} async-done(((bf16[16,1024]{1,0:T(8,128)(2,1)}), bf16[512,1024]{1,0:T(8,128)(2,1)}) %all-gather.5.cloned.1.call-update) | async-done | bytes 1048592 | tf_op jit(solution)/shard_map/all_gather | solution.py:69
  288.2 10.8 %collective-permute-done.2 = bf16[2,6,12,1024]{3,2,1,0:T(8,128)(2,1)S(1)} collective-permute-done((bf16[2,6,12,1024]{3,2,1,0:T(8,128)(2,1)S(1)}, bf16[2,6,12,1024]{3,2,1,0:T(8,128)(2,1)S(1)}, u32[]{:S(2)}, u32[]{:S(2)}) %collective-permute-start.2) | collective-permute-done | bytes 294944 | tf_op jit(solution)/shard_map/ppermute | solution.py:19
  299.2 2.2 collective-permute-start.3
  301.4 9.7 %collective-permute-done.3 = bf16[2,12,6,1024]{3,2,1,0:T(8,128)(2,1)S(1)} collective-permute-done((bf16[2,12,6,1024]{3,2,1,0:T(8,128)(2,1)S(1)}, bf16[2,12,6,1024]{3,2,1,0:T(8,128)(2,1)S(1)}, u32[]{:S(2)}, u32[]{:S(2)}) %collective-permute-start.3) | collective-permute-done | bytes 294944 | tf_op jit(solution)/shard_map/ppermute | solution.py:19
  312.6 2.2 fusion.25
  315.0 2.1 collective-permute-start.4
  317.1 7.6 %collective-permute-done.4 = bf16[2,12,6,1024]{3,2,1,0:T(8,128)(2,1)S(1)} collective-permute-done((bf16[2,12,6,1024]{3,2,1,0:T(8,128)(2,1)S(1)}, bf16[2,12,6,1024]{3,2,1,0:T(8,128)(2,1)S(1)}, u32[]{:S(2)}, u32[]{:S(2)}) %collective-permute-start.4) | collective-permute-done | bytes 294944 | tf_op jit(solution)/shard_map/ppermute | solution.py:19
  324.9 5.9 %collective-permute-start.5 = (bf16[2,6,12,1024]{3,2,1,0:T(8,128)(2,1)S(1)}, bf16[2,6,12,1024]{3,2,1,0:T(8,128)(2,1)S(1)}, u32[]{:S(2)}, u32[]{:S(2)}) collective-permute-start(bf16[2,6,12,1024]{3,2,1,0:T(8,128)(2,1)S(1)} %get-tuple-element.13), channel_id=1, source_target_pairs={{0,480},{32,0},{64,32},{96,64},{128,96},{160,128},{192,160},{224,1... | collective-permute-start | bytes 884744 | tf_op jit(solution)/shard_map/ppermute | solution.py:19
  330.9 5.1 %collective-permute-done.5 = bf16[2,6,12,1024]{3,2,1,0:T(8,128)(2,1)S(1)} collective-permute-done((bf16[2,6,12,1024]{3,2,1,0:T(8,128)(2,1)S(1)}, bf16[2,6,12,1024]{3,2,1,0:T(8,128)(2,1)S(1)}, u32[]{:S(2)}, u32[]{:S(2)}) %collective-permute-start.5) | collective-permute-done | bytes 294944 | tf_op jit(solution)/shard_map/ppermute | solution.py:19
  339.0 2.6 convolution_convert_fusion.5
  343.5 2.5 fusion.31
  346.0 2.4 fusion.39
  348.5 5.0 %fusion.32 = bf16[1,288,1,8,64]{1,4,3,2,0:T(8,128)(2,1)} fusion(bf16[8,288,288]{1,2,0:T(8,128)(2,1)S(1)} %divide_convert_fusion, f32[8,288,288]{1,2,0:T(8,128)} %fusion.39, bf16[1,288,3,8,64]{1,4,3,2,0:T(8,128)(2,1)S(1)} %bitcast.53), kind=kOutput, calls=%fused_computation.47 | convolution fusion | flops 89729568 | bytes 11304960 | tf_op jit(solution)/shard_map/whqk,wqhe->wkhe/dot_general | solution.py:124
  353.4 4.9 %fusion.33 = bf16[1,288,1,8,64]{1,4,3,2,0:T(8,128)(2,1)} fusion(bf16[8,288,288]{1,2,0:T(8,128)(2,1)S(1)} %divide_convert_fusion, f32[8,288,288]{1,2,0:T(8,128)} %fusion.39, bf16[1,288,3,8,64]{1,4,3,2,0:T(8,128)(2,1)S(1)} %bitcast.54), kind=kOutput, calls=%fused_computation.48 | convolution fusion | flops 89729568 | bytes 11304960 | tf_op jit(solution)/shard_map/whqk,wkhe->wqhe/dot_general | solution.py:121
  359.8 3.4 convolution_convert_fusion.1
  365.5 11.0 %collective-permute-done.6 = bf16[2,6,12,1024]{3,2,1,0:T(8,128)(2,1)S(1)} collective-permute-done((bf16[2,6,12,1024]{3,2,1,0:T(8,128)(2,1)S(1)}, bf16[2,6,12,1024]{3,2,1,0:T(8,128)(2,1)S(1)}, u32[]{:S(2)}, u32[]{:S(2)}) %collective-permute-start.6) | collective-permute-done | bytes 294944 | tf_op jit(solution)/shard_map/ppermute | solution.py:19
  376.6 2.1 collective-permute-start.7
  380.1 8.3 %collective-permute-done.7 = bf16[2,12,6,1024]{3,2,1,0:T(8,128)(2,1)S(1)} collective-permute-done((bf16[2,12,6,1024]{3,2,1,0:T(8,128)(2,1)S(1)}, bf16[2,12,6,1024]{3,2,1,0:T(8,128)(2,1)S(1)}, u32[]{:S(2)}, u32[]{:S(2)}) %collective-permute-start.7) | collective-permute-done | bytes 294944 | tf_op jit(solution)/shard_map/ppermute | solution.py:19
  (54 shorter events, 28.6 us)
Async XLA Ops:
  7.2 145.0 %all-gather.3.cloned.1.call-start = ((), (), s32[]{:S(2)}) async-start(), calls=%async_computation | async-start | bytes 3244032 | tf_op jit(solution)/shard_map/all_gather | solution.py:68
  7.9 274.3 %all-gather.5.cloned.1.call-start = ((), (), s32[]{:S(2)}) async-start(), calls=%async_computation.1 | async-start | bytes 1081344 | tf_op jit(solution)/shard_map/all_gather | solution.py:69
  9.4 18.3 %collective-permute-start = (bf16[2,12,6,1024]{3,0,2,1:T(2,128)(2,1)S(1)}, bf16[2,12,6,1024]{3,0,2,1:T(2,128)(2,1)S(1)}, u32[]{:S(2)}, u32[]{:S(2)}) collective-permute-start(bf16[2,12,6,1024]{3,0,2,1:T(2,128)(2,1)S(1)} %get-tuple-element.21), channel_id=1, source_target_pairs={{0,31},{1,0},{2,1},{3,2},{4,3},{5,4},{6,5},{7,6},{8,7},{9,8},{10,9... | collective-permute-start | bytes 884744 | tf_op jit(solution)/shard_map/ppermute | solution.py:19
  28.5 9.8 %collective-permute-start.1 = (bf16[2,6,12,1024]{3,0,2,1:T(2,128)(2,1)S(1)}, bf16[2,6,12,1024]{3,0,2,1:T(2,128)(2,1)S(1)}, u32[]{:S(2)}, u32[]{:S(2)}) collective-permute-start(bf16[2,6,12,1024]{3,0,2,1:T(2,128)(2,1)S(1)} %get-tuple-element.19), channel_id=1, source_target_pairs={{0,480},{32,0},{64,32},{96,64},{128,96},{160,128},{192,160},{224,1... | collective-permute-start | bytes 884744 | tf_op jit(solution)/shard_map/ppermute | solution.py:19
  286.3 12.7 %collective-permute-start.2 = (bf16[2,6,12,1024]{3,2,1,0:T(8,128)(2,1)S(1)}, bf16[2,6,12,1024]{3,2,1,0:T(8,128)(2,1)S(1)}, u32[]{:S(2)}, u32[]{:S(2)}) collective-permute-start(bf16[2,6,12,1024]{3,2,1,0:T(8,128)(2,1)S(1)} %get-tuple-element.16), channel_id=1, source_target_pairs={{0,32},{32,64},{64,96},{96,128},{128,160},{160,192},{192,224},{224... | collective-permute-start | bytes 884744 | tf_op jit(solution)/shard_map/ppermute | solution.py:19
  299.0 12.9 %copy-start = (bf16[2,12,12,1024]{3,0,2,1:T(2,128)(2,1)S(1)}, bf16[2,12,12,1024]{3,0,2,1:T(2,128)(2,1)}, u32[]{:S(2)}) copy-start(bf16[2,12,12,1024]{3,0,2,1:T(2,128)(2,1)} %param.11) | copy-start | bytes 1769476
  299.0 12.9 %copy-start.4 = (f32[1024]{0:T(1024)S(1)}, f32[1024]{0:T(1024)}, u32[]{:S(2)}) copy-start(f32[1024]{0:T(1024)} %param.9) | copy-start | bytes 12292
  299.2 13.4 %copy-start.3 = (bf16[2,12,12,1024]{3,0,2,1:T(2,128)(2,1)S(1)}, bf16[2,12,12,1024]{3,0,2,1:T(2,128)(2,1)}, u32[]{:S(2)}) copy-start(bf16[2,12,12,1024]{3,0,2,1:T(2,128)(2,1)} %param.6) | copy-start | bytes 1769476
  299.2 13.4 %copy-start.5 = (f32[1024]{0:T(1024)S(1)}, f32[1024]{0:T(1024)}, u32[]{:S(2)}) copy-start(f32[1024]{0:T(1024)} %param.10) | copy-start | bytes 12292
  299.2 11.9 %collective-permute-start.3 = (bf16[2,12,6,1024]{3,2,1,0:T(8,128)(2,1)S(1)}, bf16[2,12,6,1024]{3,2,1,0:T(8,128)(2,1)S(1)}, u32[]{:S(2)}, u32[]{:S(2)}) collective-permute-start(bf16[2,12,6,1024]{3,2,1,0:T(8,128)(2,1)S(1)} %fusion.38), channel_id=1, source_target_pairs={{0,1},{1,2},{2,3},{3,4},{4,5},{5,6},{6,7},{7,8},{8,9},{9,10},{10,1... | collective-permute-start | bytes 884744 | tf_op jit(solution)/shard_map/ppermute | solution.py:19
  315.0 9.7 %collective-permute-start.4 = (bf16[2,12,6,1024]{3,2,1,0:T(8,128)(2,1)S(1)}, bf16[2,12,6,1024]{3,2,1,0:T(8,128)(2,1)S(1)}, u32[]{:S(2)}, u32[]{:S(2)}) collective-permute-start(bf16[2,12,6,1024]{3,2,1,0:T(8,128)(2,1)S(1)} %get-tuple-element.15), channel_id=1, source_target_pairs={{0,31},{1,0},{2,1},{3,2},{4,3},{5,4},{6,5},{7,6},{8,7},{9,8},{10,9... | collective-permute-start | bytes 884744 | tf_op jit(solution)/shard_map/ppermute | solution.py:19
  324.9 11.0 %collective-permute-start.5 = (bf16[2,6,12,1024]{3,2,1,0:T(8,128)(2,1)S(1)}, bf16[2,6,12,1024]{3,2,1,0:T(8,128)(2,1)S(1)}, u32[]{:S(2)}, u32[]{:S(2)}) collective-permute-start(bf16[2,6,12,1024]{3,2,1,0:T(8,128)(2,1)S(1)} %get-tuple-element.13), channel_id=1, source_target_pairs={{0,480},{32,0},{64,32},{96,64},{128,96},{160,128},{192,160},{224,1... | collective-permute-start | bytes 884744 | tf_op jit(solution)/shard_map/ppermute | solution.py:19
  343.5 2.5 copy-start.1
  363.2 15.5 %copy-start.2 = (bf16[2,12,12,1024]{3,2,1,0:T(8,128)(2,1)S(1)}, bf16[2,12,12,1024]{3,2,1,0:T(8,128)(2,1)}, u32[]{:S(2)}) copy-start(bf16[2,12,12,1024]{3,2,1,0:T(8,128)(2,1)} %get-tuple-element.9) | copy-start | bytes 1769476
  363.4 13.0 %collective-permute-start.6 = (bf16[2,6,12,1024]{3,2,1,0:T(8,128)(2,1)S(1)}, bf16[2,6,12,1024]{3,2,1,0:T(8,128)(2,1)S(1)}, u32[]{:S(2)}, u32[]{:S(2)}) collective-permute-start(bf16[2,6,12,1024]{3,2,1,0:T(8,128)(2,1)S(1)} %get-tuple-element.10), channel_id=1, source_target_pairs={{0,32},{32,64},{64,96},{96,128},{128,160},{160,192},{192,224},{224... | collective-permute-start | bytes 884744 | tf_op jit(solution)/shard_map/ppermute | solution.py:19
  376.6 11.8 %collective-permute-start.7 = (bf16[2,12,6,1024]{3,2,1,0:T(8,128)(2,1)S(1)}, bf16[2,12,6,1024]{3,2,1,0:T(8,128)(2,1)S(1)}, u32[]{:S(2)}, u32[]{:S(2)}) collective-permute-start(bf16[2,12,6,1024]{3,2,1,0:T(8,128)(2,1)S(1)} %fusion.36), channel_id=1, source_target_pairs={{0,1},{1,2},{2,3},{3,4},{4,5},{5,6},{6,7},{7,8},{8,9},{9,10},{10,1... | collective-permute-start | bytes 884744 | tf_op jit(solution)/shard_map/ppermute | solution.py:19
Sparse Core Ops, SparseCore 0:
  10.1 142.0 all-gather.2
  154.2 127.9 all-gather.4
where the time goes:
time: 398 us; the launch traced here: 397 us
  waiting for transfers between devices  301 us (76%)
  starting transfers between devices  32.1 us (8%)
  matrix products  27.6 us (7%)
  between operations  14.3 us (4%)
  local copies, waits for them, and re-layouts  12 us (3%)
  other arithmetic  10.3 us (3%)
    all_gather x1, waiting for transfers between devices, per_device(): lax.all_gather(out_weight, 'lon', axis=0, tiled=True)  123 us
    all_gather x1, waiting for transfers between devices, per_device(): lax.all_gather(qkv_weight, 'lon', axis=0, tiled=True)  113 us
    ppermute x8, waiting for transfers between devices, from_behind(): lax.ppermute(shard, axis, [(i, (i + by) % size) for i in range(size)])  64.3 us
    ppermute x8, starting transfers between devices, from_behind(): lax.ppermute(shard, axis, [(i, (i + by) % size) for i in range(size)])  32.1 us
  transfers between devices with their start and end apart: 10, of which 10 were waited for; matrix products, arithmetic and copies ran while one was open for 3% of the time, Pallas kernels for 0%

commit v1 on v0

v1 whole, which is shorter than its diff:
```python
import functools

import jax
import jax.numpy as jnp
from jax import lax
from jax.experimental import pallas as pl
from jax.experimental.pallas import tpu as pltpu
from jax.sharding import PartitionSpec as P

MESH = pl.DeviceIdType.MESH
BF = jnp.bfloat16
F32 = jnp.float32

D = 1024
HEADS = 8
HEAD_DIM = 64
LEV = 2
WIN = 12
INNER = 512
HALF = 6
TOK = LEV * WIN * WIN
QUARTER = TOK // 4
PIECE = 80
GROUP = 4
GW = GROUP * HEAD_DIM
CHUNK = 32
STEPS = TOK // CHUNK
LANES = GROUP * CHUNK
EPS = 1e-05

SENT = (64, 144, 208)


def nt(a, b):
    return lax.dot_general(a, b, (((1,), (1,)), ((), ())), preferred_element_type=F32)


def nn(a, b):
    return lax.dot_general(a, b, (((1,), (0,)), ((), ())), preferred_element_type=F32)


def tn(a, b):
    return lax.dot_general(a, b, (((0,), (0,)), ((), ())), preferred_element_type=F32)


def ds(start, size):
    return pl.ds(pl.multiple_of(start, size), size)


def kernel(
    n_lat, n_lon,
    t_ref, g_ref, wq_ref, wo_ref, gain_ref, bias_ref,
    m_out, d_out,
    wqf, wof, land_t, land_g, xw, gw, packed, heads, attn, agrad, hgrad, pgrad,
    pt, dst, qblk, doblk, mixed, tgrad,
    own_sem, zs, zr, xs, xr, ss, sr, hs, hr,
):
    lat, lon = lax.axis_index("lat"), lax.axis_index("lon")
    nz = n_lon // 2
    ns = nz // 2
    rq, ro = D // n_lon, INNER // n_lon
    core, par, z = lax.rem(lat, 2), lax.rem(lon, 2), lon // 2
    lat_lo, lat_hi = lax.rem(lat + n_lat - 1, n_lat), lax.rem(lat + 1, n_lat)
    lon_lo, lon_hi = lax.rem(lon + n_lon - 1, n_lon), lax.rem(lon + 1, n_lon)
    sib = (lat + 1 - 2 * core, lon)
    up = (lat, lax.rem(lon + 2, n_lon))
    down = (lat, lax.rem(lon + n_lon - 2, n_lon))
    differ = lax.rem(par + core, 2)
    across = lon + 1 - 2 * par
    x_to = (lax.rem(lat + differ * (n_lat // 2), n_lat), across)
    x_from = (lax.rem(lat + (1 - differ) * (n_lat // 2), n_lat), across)
    west, north, diag = (lat, lon_lo), (lat_lo, lon), (lat_lo, lon_lo)
    east, south, far = (lat, lon_hi), (lat_hi, lon), (lat_hi, lon_hi)

    barrier = pltpu.get_barrier_semaphore()
    met = (sib, up, down, x_to, x_from, west, north, diag, east, south, far)
    for who in met:
        pl.semaphore_signal(barrier, inc=1, device_id=who, device_id_type=MESH)
    pl.semaphore_wait(barrier, len(met))

    def remote(src, dst, send, recv, who):
        return pltpu.make_async_remote_copy(
            src_ref=src, dst_ref=dst, send_sem=send, recv_sem=recv, device_id=who, device_id_type=MESH
        )

    def halo_in(field, src, land):
        return [
            remote(src.at[pl.ds(SENT[k], PIECE), :], land.at[k], hs.at[field * 3 + k], hr.at[field * 3 + k], who)
            for k, who in enumerate((west, north, diag))
        ]

    in_t = halo_in(0, t_ref, land_t)
    in_g = halo_in(1, g_ref, land_g)
    for copy in in_t:
        copy.start()

    def piece(kind, zq, p, c):
        if kind == 0:
            return wqf.at[ds((zq * 2 + p) * rq + c * (rq // 2), rq // 2), :]
        return wof.at[ds((zq * 2 + p) * ro, ro), ds(c * (D // 2), D // 2)]

    def own_piece(kind):
        if kind == 0:
            return wq_ref.at[ds(core * (rq // 2), rq // 2), :]
        return wo_ref.at[:, ds(core * (D // 2), D // 2)]

    def z_copy(kind, way, s, zq, src=None):
        dst = piece(kind, zq, par, core)
        i = (way * (ns + 1) + s) * 2 + kind
        return remote(dst if src is None else src, dst, zs.at[i], zr.at[i], (up, down)[way])

    def x_copy(kind, d, zq, p, src=None):
        dst = piece(kind, zq, p, core)
        i = d * 2 + kind
        return remote(dst if src is None else src, dst, xs.at[i], xr.at[i], x_to)

    def s_copy(kind, other, d, zq, c):
        ref = piece(kind, zq, lax.rem(par + other, 2), c)
        i = (other * nz + d) * 2 + kind
        return remote(ref, ref, ss.at[i], sr.at[i], sib)

    def ahead(zq, s):
        return lax.rem(zq + s, nz)

    def behind(zq, s):
        return lax.rem(zq - s + nz, nz)

    local = [
        pltpu.make_async_copy(wq_ref, wqf.at[ds(lon * rq, rq), :], own_sem.at[0]),
        pltpu.make_async_copy(wo_ref, wof.at[ds(lon * ro, ro), :], own_sem.at[1]),
    ]
    for kind in (0, 1):
        src = own_piece(kind)
        z_copy(kind, 0, 1, z, src).start()
        if ns > 1:
            z_copy(kind, 1, 1, z, src).start()
        x_copy(kind, 0, z, par, src).start()
    for copy in local:
        copy.start()
    for copy in in_g:
        copy.start()

    def z_arrive(kind, way, s, last):
        zq, d = (behind(z, s), s) if way == 0 else (ahead(z, s), nz - s)
        z_copy(kind, way, s, zq).wait_recv()
        if not last:
            z_copy(kind, way, s + 1, zq).start()
        x_copy(kind, d, zq, par).start()
        s_copy(kind, 0, d, zq, core).start()

    def x_arrive(kind, d):
        zq = behind(z, d)
        x_copy(kind, d, zq, 1 - par).wait_recv()
        s_copy(kind, 1, d, zq, core).start()

    def z_step(s, up_last, down_in, down_last):
        for kind in (0, 1):
            z_arrive(kind, 0, s, up_last)
            if down_in:
                z_arrive(kind, 1, s, down_last)

    def x_step(s, both):
        for kind in (0, 1):
            x_arrive(kind, s)
            if both:
                x_arrive(kind, nz - s)

    def fixed_step(s):
        z_step(s, s == ns, s < ns, s == ns - 1)
        x_step(s - 1, s > 1)

    fixed_step(1)
    if ns > 3:
        def middle(s, carry):
            z_step(s, False, True, False)
            x_step(s - 1, True)
            return carry

        lax.fori_loop(2, ns - 1, middle, 0)
    for s in range(max(2, ns - 1), ns + 1):
        fixed_step(s)
    x_step(ns, False)

    def assemble(own, land, dst):
        row = lax.broadcasted_iota(jnp.int32, (16, D), 0)
        dst[0:64, :] = own[0:64, :]
        dst[64:80, :] = jnp.where(row < 8, own[64:80, :].astype(F32), land[0, 0:16, :].astype(F32)).astype(BF)
        dst[80:144, :] = land[0, 16:80, :]
        dst[144:208, :] = land[1, 0:64, :]
        dst[208:224, :] = jnp.where(row < 8, land[1, 64:80, :].astype(F32), land[2, 0:16, :].astype(F32)).astype(BF)
        dst[224:288, :] = land[2, 16:80, :]

    for copy in in_t:
        copy.wait_recv()
    assemble(t_ref, land_t, xw)

    def s_wait(d, carry):
        for kind in (0, 1):
            s_copy(kind, 0, d, behind(z, d), 1 - core).wait_recv()
            s_copy(kind, 1, d, behind(z, d), 1 - core).wait_recv()
        return carry

    for kind in (0, 1):
        s_copy(kind, 1, 0, z, 1 - core).wait_recv()
    lax.fori_loop(1, nz, s_wait, 0)
    for copy in local:
        copy.wait()

    def project(n, carry):
        cols = ds(n * 256, 256)
        packed[:, cols] = nn(xw[...], wqf[:, cols]).astype(BF)
        return carry

    lax.fori_loop(0, 3 * INNER // 256, project, 0)

    lane_head = lax.broadcasted_iota(jnp.int32, (CHUNK, GW), 1) // HEAD_DIM
    head_mask = [(lane_head == h).astype(F32).astype(BF) for h in range(GROUP)]
    banned = jnp.where(lat == n_lat - 1, -1e30, 0.0).astype(F32)
    lane_query = lax.rem(lax.broadcasted_iota(jnp.int32, (1, LANES), 1), CHUNK)

    def spread(rows):
        return jnp.concatenate([rows * m for m in head_mask], axis=0)

    def gather_heads(wide):
        out = wide[0:CHUNK, :]
        for h in range(1, GROUP):
            out = jnp.where(lane_head == h, wide[h * CHUNK : (h + 1) * CHUNK, :], out)
        return out

    for g in range(HEADS // GROUP):
        q_at, k_at, v_at = g * GW, INNER + g * GW, 2 * INNER + g * GW

        def forward(c, carry, g=g, q_at=q_at, k_at=k_at, v_at=v_at):
            rows, cols = ds(c * CHUNK, CHUNK), ds(c * LANES, LANES)
            q = spread(packed[rows, q_at : q_at + GW])
            qblk[g, cols, :] = q
            s = nt(packed[:, k_at : k_at + GW], q)
            side = ((c * CHUNK + lane_query) >= TOK // 2).astype(F32)
            s = jnp.concatenate([s[: TOK // 2] + side * banned, s[TOK // 2 :] + (1.0 - side) * banned], axis=0)
            top = jnp.max(s, axis=0, keepdims=True)
            e = jnp.exp((s - top) * (HEAD_DIM ** -0.5))
            p = (e * (1.0 / jnp.sum(e, axis=0, keepdims=True))).astype(BF)
            pt[g, :, cols] = p
            o = tn(p, packed[:, v_at : v_at + GW])
            heads[rows, q_at : q_at + GW] = gather_heads(o).astype(BF)
            return carry

        lax.fori_loop(0, STEPS, forward, 0)

    def out_project(n, carry):
        cols = ds(n * 256, 256)
        attn[:, cols] = nn(heads[...], wof[:, cols]).astype(BF)
        return carry

    lax.fori_loop(0, D // 256, out_project, 0)

    for copy in in_g:
        copy.wait_recv()
    assemble(g_ref, land_g, gw)

    def norm(c, carry):
        rows = ds(c * CHUNK, CHUNK)
        a = attn[rows, :].astype(F32)
        centered = a - jnp.mean(a, axis=-1, keepdims=True)
        inverse = lax.rsqrt(jnp.mean(centered * centered, axis=-1, keepdims=True) + EPS)
        normed = centered * inverse
        gain = gain_ref[...]
        mixed[rows, :] = (xw[rows, :].astype(F32) + normed * gain + bias_ref[...]).astype(BF)
        scaled = gw[rows, :].astype(F32) * gain
        back = scaled - jnp.mean(scaled, axis=-1, keepdims=True)
        back = back - normed * jnp.mean(scaled * normed, axis=-1, keepdims=True)
        agrad[rows, :] = (back * inverse).astype(BF)
        return carry

    lax.fori_loop(0, TOK // CHUNK, norm, 0)

    def halo_out(field, src, out):
        copies = [
            remote(
                src.at[pl.ds(SENT[k], PIECE), :], out.at[k + 1],
                hs.at[(field + 2) * 3 + k], hr.at[(field + 2) * 3 + k], who,
            )
            for k, who in enumerate((east, south, far))
        ]
        keep = pltpu.make_async_copy(src.at[pl.ds(0, PIECE), :], out.at[0], own_sem.at[2 + field])
        for copy in copies:
            copy.start()
        keep.start()
        return copies, keep

    out_m = halo_out(0, mixed, m_out)

    def back_project(n, carry):
        cols = ds(n * 256, 256)
        hgrad[:, cols] = nt(agrad[...], wof[cols, :]).astype(BF)
        return carry

    lax.fori_loop(0, INNER // 256, back_project, 0)

    for g in range(HEADS // GROUP):
        q_at, k_at, v_at = g * GW, INNER + g * GW, 2 * INNER + g * GW

        def backward(c, carry, g=g, q_at=q_at, k_at=k_at, v_at=v_at):
            rows, cols = ds(c * CHUNK, CHUNK), ds(c * LANES, LANES)
            do = spread(hgrad[rows, q_at : q_at + GW])
            doblk[cols, :] = do
            dp = nt(packed[:, v_at : v_at + GW], do)
            p = pt[g, :, cols].astype(F32)
            total = jnp.sum(p * dp, axis=0, keepdims=True)
            dscore = (p * (dp - total) * (HEAD_DIM ** -0.5)).astype(BF)
            dst[:, cols] = dscore
            dq = tn(dscore, packed[:, k_at : k_at + GW])
            pgrad[rows, q_at : q_at + GW] = gather_heads(dq).astype(BF)
            return carry

        lax.fori_loop(0, STEPS, backward, 0)
        pgrad[:, v_at : v_at + GW] = nn(pt[g], doblk[...]).astype(BF)
        pgrad[:, k_at : k_at + GW] = nn(dst[...], qblk[g]).astype(BF)

    def unproject(n, carry):
        cols = ds(n * 256, 256)
        sg = nt(pgrad[...], wqf[cols, :]).astype(BF).astype(F32)
        tgrad[:, cols] = (gw[:, cols].astype(F32) + sg).astype(BF)
        return carry

    lax.fori_loop(0, D // 256, unproject, 0)
    out_d = halo_out(1, tgrad, d_out)

    for kind in (0, 1):
        z_copy(kind, 0, 1, z).wait_send()
        x_copy(kind, 0, z, par).wait_send()
        s_copy(kind, 1, 0, z, core).wait_send()

    def sent(d, carry):
        for kind in (0, 1):
            x_copy(kind, d, behind(z, d), par).wait_send()
            s_copy(kind, 0, d, behind(z, d), core).wait_send()
            s_copy(kind, 1, d, behind(z, d), core).wait_send()
        return carry

    lax.fori_loop(1, nz, sent, 0)

    def sent_z(s, carry):
        for kind in (0, 1):
            z_copy(kind, 0, s, behind(z, s - 1)).wait_send()
            z_copy(kind, 1, s - 1, ahead(z, s - 2)).wait_send()
        return carry

    lax.fori_loop(2, ns + 1, sent_z, 0)
    for copy in in_t + in_g:
        copy.wait_send()
    for copies, keep in (out_m, out_d):
        keep.wait()
        for copy in copies:
            copy.wait()


def per_device(n_lat, n_lon, tokens, qkv_weight, out_weight, norm_gain, norm_bias, mixed_grad):
    def quarters(field):
        cut = field.reshape(LEV, 2, HALF, 2, HALF, D)
        return jnp.concatenate(
            [cut[:, i, :, j].reshape(QUARTER, D) for i, j in ((1, 1), (1, 0), (0, 1), (0, 0))], axis=0
        )

    def join(pieces):
        own, left, above, corner = (
            pieces[k, 8 * (k % 2) : 8 * (k % 2) + QUARTER].reshape(LEV, HALF, HALF, D) for k in range(4)
        )
        return jnp.concatenate(
            [jnp.concatenate([corner, above], axis=2), jnp.concatenate([left, own], axis=2)], axis=1
        )

    nz = n_lon // 2
    ns = nz // 2
    vmem = pl.BlockSpec(memory_space=pltpu.VMEM)
    m_out, d_out = pl.pallas_call(
        functools.partial(kernel, n_lat, n_lon),
        out_shape=[jax.ShapeDtypeStruct((4, PIECE, D), BF)] * 2,
        in_specs=[vmem] * 6,
        out_specs=[pl.BlockSpec(memory_space=pl.ANY)] * 2,
        scratch_shapes=[
            pltpu.VMEM((D, 3 * INNER), BF),
            pltpu.VMEM((INNER, D), BF),
            pltpu.VMEM((3, PIECE, D), BF),
            pltpu.VMEM((3, PIECE, D), BF),
            pltpu.VMEM((TOK, D), BF),
            pltpu.VMEM((TOK, D), BF),
            pltpu.VMEM((TOK, 3 * INNER), BF),
            pltpu.VMEM((TOK, INNER), BF),
            pltpu.VMEM((TOK, D), BF),
            pltpu.VMEM((TOK, D), BF),
            pltpu.VMEM((TOK, INNER), BF),
            pltpu.VMEM((TOK, 3 * INNER), BF),
            pltpu.VMEM((2, TOK, GROUP * TOK), BF),
            pltpu.VMEM((TOK, GROUP * TOK), BF),
            pltpu.VMEM((2, GROUP * TOK, GW), BF),
            pltpu.VMEM((GROUP * TOK, GW), BF),
            pltpu.VMEM((TOK, D), BF),
            pltpu.VMEM((TOK, D), BF),
            pltpu.SemaphoreType.DMA((4,)),
            pltpu.SemaphoreType.DMA((4 * (ns + 1),)),
            pltpu.SemaphoreType.DMA((4 * (ns + 1),)),
            pltpu.SemaphoreType.DMA((2 * nz,)),
            pltpu.SemaphoreType.DMA((2 * nz,)),
            pltpu.SemaphoreType.DMA((4 * nz,)),
            pltpu.SemaphoreType.DMA((4 * nz,)),
            pltpu.SemaphoreType.DMA((12,)),
            pltpu.SemaphoreType.DMA((12,)),
        ],
        compiler_params=pltpu.CompilerParams(
            collective_id=0, has_side_effects=True, vmem_limit_bytes=40 * 1024 * 1024
        ),
    )(
        quarters(tokens), quarters(mixed_grad), qkv_weight, out_weight,
        norm_gain.reshape(1, D), norm_bias.reshape(1, D),
    )
    return join(m_out), join(d_out)


def solution(mesh):
    placed = (
        P(None, "lat", "lon", None),
        P("lon", None),
        P("lon", None),
        P(),
        P(),
        P(None, "lat", "lon", None),
    )
    return jax.shard_map(
        functools.partial(per_device, mesh.shape["lat"], mesh.shape["lon"]),
        mesh=mesh,
        in_specs=placed,
        out_specs=(P(None, "lat", "lon", None), P(None, "lat", "lon", None)),
        check_vma=False,
    )
```

time: 398 us -> 105 us (0.26)
  the two profiles are of different devices: /device:TPU:4 before, /device:TPU:1 now
where the time goes in v1:
time: 105 us; the launch traced here: 104 us
  Pallas kernels  94.4 us (90%)
  local copies, waits for them, and re-layouts  7.79 us (7%)
    pallas_call x1, Pallas kernels, per_device(): pl.pallas_call(functools.partial(kernel, n_lat, n_lon), out_shape=[jax.Sh...  94.4 us
    unnamed x20, local copies, waits for them, and re-layouts  4.85 us

profile of v1, /device:TPU:1, one launch (start us, length us, event | category | flops | bytes accessed | tf_op | source)
XLA Modules:
  0.0 103.7 jit_solution(10916391836864712903)
XLA Ops:
  0.6 1.6 %fusion.3 = (bf16[2,1,6,1,6,1024]{5,0,4,3,2,1:T(2,128)(2,1)S(1)}, bf16[2,1,6,1,6,1024]{5,0,4,3,2,1:T(2,128)(2,1)S(1)}, bf16[2,1,6,1,6,1024]{5,0,4,3,2,1:T(2,128)(2,1)S(1)}, bf16[2,1,6,1,6,1024]{5,0,4,3,2,1:T(2,128)(2,1)S(1)}) fusion(bf16[2,2,6,2,6,1024]{5,0,4,3,2,1:T(2,128)(2,1)} %bitcast.22), kind=kLoop, calls=%fused_computation.7 | loop fusion | bytes 1179648 | tf_op jit(solution)/shard_map/slice | solution.py:362
  2.2 0.1 reshape_squeeze.48
  2.3 0.1 reshape_squeeze.50
  2.5 0.1 reshape_squeeze.49
  2.6 0.1 reshape_squeeze.51
  2.7 0.9 copy-done.4
  3.6 0.4 fusion.2
  4.1 0.1 reshape_squeeze.52
  4.2 0.1 reshape_squeeze.54
  4.3 0.1 reshape_squeeze.53
  4.5 0.1 reshape_squeeze.55
  4.6 0.7 copy-done
  5.3 94.4 %shard_map.77 = (bf16[4,80,1024]{2,1,0:T(8,128)(2,1)S(1)}, bf16[4,80,1024]{2,1,0:T(8,128)(2,1)S(1)}) custom-call(bf16[288,1024]{1,0:T(8,128)(2,1)S(1)} %pad_maximum_fusion.t_ref, bf16[288,1024]{1,0:T(8,128)(2,1)S(1)} %pad_maximum_fusion.1.g_ref, bf16[32,1536]{1,0:T(8,128)(2,1)S(1)} %copy-done, bf16[16,1024]{1,0:T(8,128)(2,1)S(1)} %copy-done.1, ...), custom_call_target="tpu_custom_call" | custom-call | tf_op jit(solution)/shard_map/pallas_call | solution.py:376
  99.7 0.1 fusion
  99.8 0.1 reshape_squeeze.60
  99.9 0.1 reshape_squeeze.63
  100.0 0.1 reshape_squeeze.62
  100.0 0.1 reshape_squeeze.61
  100.1 0.3 maximum_maximum_fusion.1
  100.4 1.4 %copy.33 = bf16[2,12,12,1024]{3,0,2,1:T(2,128)(2,1)} copy(bf16[2,12,12,1024]{3,2,1,0:T(8,128)(2,1)S(1)} %maximum_maximum_fusion.1) | data formatting | bytes 1179648
  101.8 0.1 reshape_squeeze.58
  102.0 0.1 reshape_squeeze.56
  102.0 0.3 maximum_maximum_fusion
  102.3 1.4 %copy.32 = bf16[2,12,12,1024]{3,0,2,1:T(2,128)(2,1)} copy(bf16[2,12,12,1024]{3,2,1,0:T(8,128)(2,1)S(1)} %maximum_maximum_fusion) | data formatting | bytes 1179648
  (20 shorter events, 0.5 us)
Async XLA Ops:
  2.6 1.1 %copy-start.4 = (bf16[2,12,12,1024]{3,0,2,1:T(2,128)(2,1)S(1)}, bf16[2,12,12,1024]{3,0,2,1:T(2,128)(2,1)}, u32[]{:S(2)}) copy-start(bf16[2,12,12,1024]{3,0,2,1:T(2,128)(2,1)} %param.11) | copy-start | bytes 1769476
  4.4 0.9 copy-start
  4.4 0.9 copy-start.1
  4.5 0.9 copy-start.2
  4.5 0.9 copy-start.3

commit v2 on v1

v2 whole, which is shorter than its diff:
```python
import functools

import jax
import jax.numpy as jnp
from jax import lax
from jax.experimental import pallas as pl
from jax.experimental.pallas import tpu as pltpu
from jax.sharding import PartitionSpec as P

MESH = pl.DeviceIdType.MESH
BF = jnp.bfloat16
F32 = jnp.float32

D = 1024
HEADS = 8
HEAD_DIM = 64
LEV = 2
WIN = 12
INNER = 512
HALF = 6
TOK = LEV * WIN * WIN
QUARTER = TOK // 4
GROUP = 4
GW = GROUP * HEAD_DIM
WIDE = GROUP * TOK
ROWS = 32
EPS = 1e-05

HALVES = ((1, 1), (1, 0), (0, 1), (0, 0))


def nt(a, b):
    return lax.dot_general(a, b, (((1,), (1,)), ((), ())), preferred_element_type=F32)


def nn(a, b):
    return lax.dot_general(a, b, (((1,), (0,)), ((), ())), preferred_element_type=F32)


def tn(a, b):
    return lax.dot_general(a, b, (((0,), (0,)), ((), ())), preferred_element_type=F32)


def ds(start, size):
    return pl.ds(pl.multiple_of(start, size), size)


def kernel(
    n_lat, n_lon,
    t_ref, g_ref, wq_ref, wo_ref, gain_hbm, bias_hbm,
    m_out, d_out,
    wqf, wof, gain_ref, bias_ref, land_t, land_g, xw, gw, packed, heads, attn, agrad, hgrad, pgrad,
    scores, pt, dst, qblk, doblk, mixed, tgrad,
    own_sem, zs, zr, xs, xr, ss, sr, hs, hr,
):
    lat, lon = lax.axis_index("lat"), lax.axis_index("lon")
    nz = n_lon // 2
    ns = nz // 2
    rq, ro = D // n_lon, INNER // n_lon
    core, par, z = lax.rem(lat, 2), lax.rem(lon, 2), lon // 2
    lat_lo, lat_hi = lax.rem(lat + n_lat - 1, n_lat), lax.rem(lat + 1, n_lat)
    lon_lo, lon_hi = lax.rem(lon + n_lon - 1, n_lon), lax.rem(lon + 1, n_lon)
    sib = (lat + 1 - 2 * core, lon)
    up = (lat, lax.rem(lon + 2, n_lon))
    down = (lat, lax.rem(lon + n_lon - 2, n_lon))
    differ = lax.rem(par + core, 2)
    across = lon + 1 - 2 * par
    x_to = (lax.rem(lat + differ * (n_lat // 2), n_lat), across)
    x_from = (lax.rem(lat + (1 - differ) * (n_lat // 2), n_lat), across)
    west, north, diag = (lat, lon_lo), (lat_lo, lon), (lat_lo, lon_lo)
    east, south, far = (lat, lon_hi), (lat_hi, lon), (lat_hi, lon_hi)

    barrier = pltpu.get_barrier_semaphore()
    met = (sib, up, down, x_to, x_from, west, north, diag, east, south, far)
    for who in met:
        pl.semaphore_signal(barrier, inc=1, device_id=who, device_id_type=MESH)
    pl.semaphore_wait(barrier, len(met))

    def remote(src, dst, send, recv, who):
        return pltpu.make_async_remote_copy(
            src_ref=src, dst_ref=dst, send_sem=send, recv_sem=recv, device_id=who, device_id_type=MESH
        )

    def quarter(ref, k):
        i, j = HALVES[k]
        return ref.at[pl.ds(i * HALF, HALF), pl.ds(j * HALF, HALF)]

    def halo_in(field, src, land):
        copies = [
            remote(quarter(src, k), land.at[k], hs.at[field * 4 + k], hr.at[field * 4 + k], who)
            for k, who in ((1, west), (2, north), (3, diag))
        ]
        return copies, pltpu.make_async_copy(quarter(src, 0), land.at[0], own_sem.at[4 + field])

    in_t = halo_in(0, t_ref, land_t)
    in_g = halo_in(1, g_ref, land_g)
    for copy in in_t[0]:
        copy.start()

    def piece(kind, zq, p, c):
        if kind == 0:
            return wqf.at[ds((zq * 2 + p) * rq + c * (rq // 2), rq // 2), :]
        return wof.at[ds((zq * 2 + p) * ro, ro), ds(c * (D // 2), D // 2)]

    def own_piece(kind):
        if kind == 0:
            return wq_ref.at[ds(core * (rq // 2), rq // 2), :]
        return wo_ref.at[:, ds(core * (D // 2), D // 2)]

    def z_copy(kind, way, s, zq, src=None):
        dst = piece(kind, zq, par, core)
        i = (way * (ns + 1) + s) * 2 + kind
        return remote(dst if src is None else src, dst, zs.at[i], zr.at[i], (up, down)[way])

    def x_copy(kind, d, zq, p, src=None):
        dst = piece(kind, zq, p, core)
        i = d * 2 + kind
        return remote(dst if src is None else src, dst, xs.at[i], xr.at[i], x_to)

    def s_copy(kind, other, d, zq, c):
        ref = piece(kind, zq, lax.rem(par + other, 2), c)
        i = (other * nz + d) * 2 + kind
        return remote(ref, ref, ss.at[i], sr.at[i], sib)

    def ahead(zq, s):
        return lax.rem(zq + s, nz)

    def behind(zq, s):
        return lax.rem(zq - s + nz, nz)

    local = [
        pltpu.make_async_copy(wq_ref, wqf.at[ds(lon * rq, rq), :], own_sem.at[0]),
        pltpu.make_async_copy(wo_ref, wof.at[ds(lon * ro, ro), :], own_sem.at[1]),
        pltpu.make_async_copy(gain_hbm, gain_ref, own_sem.at[2]),
        pltpu.make_async_copy(bias_hbm, bias_ref, own_sem.at[3]),
        in_t[1],
    ]
    for kind in (0, 1):
        src = own_piece(kind)
        z_copy(kind, 0, 1, z, src).start()
        if ns > 1:
            z_copy(kind, 1, 1, z, src).start()
        x_copy(kind, 0, z, par, src).start()
    for copy in local:
        copy.start()
    for copy in in_g[0]:
        copy.start()
    in_g[1].start()

    def z_arrive(kind, way, s, last):
        zq, d = (behind(z, s), s) if way == 0 else (ahead(z, s), nz - s)
        z_copy(kind, way, s, zq).wait_recv()
        if not last:
            z_copy(kind, way, s + 1, zq).start()
        x_copy(kind, d, zq, par).start()
        s_copy(kind, 0, d, zq, core).start()

    def x_arrive(kind, d):
        zq = behind(z, d)
        x_copy(kind, d, zq, 1 - par).wait_recv()
        s_copy(kind, 1, d, zq, core).start()

    def z_step(s, up_last, down_in, down_last):
        for kind in (0, 1):
            z_arrive(kind, 0, s, up_last)
            if down_in:
                z_arrive(kind, 1, s, down_last)

    def x_step(s, both):
        for kind in (0, 1):
            x_arrive(kind, s)
            if both:
                x_arrive(kind, nz - s)

    def fixed_step(s):
        z_step(s, s == ns, s < ns, s == ns - 1)
        x_step(s - 1, s > 1)

    fixed_step(1)
    if ns > 3:
        def middle(s, carry):
            z_step(s, False, True, False)
            x_step(s - 1, True)
            return carry

        lax.fori_loop(2, ns - 1, middle, 0)
    for s in range(max(2, ns - 1), ns + 1):
        fixed_step(s)

    def rows_of(land, field):
        for k in range(4):
            field[k * QUARTER : (k + 1) * QUARTER, :] = land[k].reshape(QUARTER, D)

    for copy in in_t[0]:
        copy.wait_recv()
    for copy in local:
        copy.wait()
    rows_of(land_t, xw)
    x_step(ns, False)

    def s_wait(d, carry):
        for kind in (0, 1):
            s_copy(kind, 0, d, behind(z, d), 1 - core).wait_recv()
            s_copy(kind, 1, d, behind(z, d), 1 - core).wait_recv()
        return carry

    for kind in (0, 1):
        s_copy(kind, 1, 0, z, 1 - core).wait_recv()
    lax.fori_loop(1, nz, s_wait, 0)

    def project(n, carry):
        cols = ds(n * 256, 256)
        packed[:, cols] = nn(xw[...], wqf[:, cols]).astype(BF)
        return carry

    lax.fori_loop(0, 3 * INNER // 256, project, 0)

    lane_head = lax.broadcasted_iota(jnp.int32, (TOK, GW), 1) // HEAD_DIM
    banned = jnp.where(lat == n_lat - 1, -1e30, 0.0).astype(F32)

    def spread(rows):
        return [rows * (lane_head[0:1] == h).astype(F32).astype(BF) for h in range(GROUP)]

    def gather_heads(wide):
        out = wide[0:TOK, :]
        for h in range(1, GROUP):
            out = jnp.where(lane_head == h, wide[h * TOK : (h + 1) * TOK, :], out)
        return out

    for g in range(HEADS // GROUP):
        q_at, k_at, v_at = g * GW, INNER + g * GW, 2 * INNER + g * GW
        for h, rows in enumerate(spread(packed[:, q_at : q_at + GW])):
            qblk[g, h * TOK : (h + 1) * TOK, :] = rows

        def score(c, carry, g=g, k_at=k_at):
            cols = ds(c * 384, 384)
            scores[:, cols] = nt(packed[:, k_at : k_at + GW], qblk[g, cols, :])
            return carry

        lax.fori_loop(0, WIDE // 384, score, 0)

        def soften(c, carry, g=g):
            cols = ds(c * 128, 128)
            query = lax.rem(c * 128 + lax.broadcasted_iota(jnp.int32, (1, 128), 1), TOK)
            side = (query >= TOK // 2).astype(F32)
            s = jnp.concatenate(
                [scores[: TOK // 2, cols] + side * banned, scores[TOK // 2 :, cols] + (1.0 - side) * banned], axis=0
            )
            top = jnp.max(s, axis=0, keepdims=True)
            e = jnp.exp((s - top) * (HEAD_DIM ** -0.5))
            pt[g, :, cols] = (e * (1.0 / jnp.sum(e, axis=0, keepdims=True))).astype(BF)
            return carry

        lax.fori_loop(0, WIDE // 128, soften, 0, unroll=3)
        heads[:, q_at : q_at + GW] = gather_heads(tn(pt[g], packed[:, v_at : v_at + GW])).astype(BF)

    def out_project(n, carry):
        cols = ds(n * 256, 256)
        attn[:, cols] = nn(heads[...], wof[:, cols]).astype(BF)
        return carry

    lax.fori_loop(0, D // 256, out_project, 0)

    for copy in in_g[0]:
        copy.wait_recv()
    in_g[1].wait()
    rows_of(land_g, gw)

    def norm(c, carry):
        rows = ds(c * ROWS, ROWS)
        a = attn[rows, :].astype(F32)
        gain = gain_ref[...]
        scaled = gw[rows, :].astype(F32) * gain
        centered = a - jnp.mean(a, axis=-1, keepdims=True)
        level = scaled - jnp.mean(scaled, axis=-1, keepdims=True)
        inverse = lax.rsqrt(jnp.mean(centered * centered, axis=-1, keepdims=True) + EPS)
        along = jnp.mean(scaled * centered, axis=-1, keepdims=True) * inverse
        normed = centered * inverse
        mixed[rows, :] = (xw[rows, :].astype(F32) + normed * gain + bias_ref[...]).astype(BF)
        agrad[rows, :] = ((level - normed * along) * inverse).astype(BF)
        return carry

    lax.fori_loop(0, TOK // ROWS, norm, 0, unroll=3)

    def halo_out(field, rows, land, out):
        for k in range(4):
            land[k] = rows[k * QUARTER : (k + 1) * QUARTER, :].reshape(HALF, HALF, LEV, D)
        copies = [
            remote(land.at[k], quarter(out, k), hs.at[(field + 2) * 4 + k], hr.at[(field + 2) * 4 + k], who)
            for k, who in ((1, east), (2, south), (3, far))
        ]
        keep = pltpu.make_async_copy(land.at[0], quarter(out, 0), own_sem.at[6 + field])
        for copy in copies:
            copy.start()
        keep.start()
        return copies, keep

    out_m = halo_out(0, mixed, land_t, m_out)

    def back_project(n, carry):
        cols = ds(n * 256, 256)
        hgrad[:, cols] = nt(agrad[...], wof[cols, :]).astype(BF)
        return carry

    lax.fori_loop(0, INNER // 256, back_project, 0)

    for g in range(HEADS // GROUP):
        q_at, k_at, v_at = g * GW, INNER + g * GW, 2 * INNER + g * GW
        for h, rows in enumerate(spread(hgrad[:, q_at : q_at + GW])):
            doblk[h * TOK : (h + 1) * TOK, :] = rows

        def prob_grad(c, carry, v_at=v_at):
            cols = ds(c * 384, 384)
            scores[:, cols] = nt(packed[:, v_at : v_at + GW], doblk[cols, :])
            return carry

        lax.fori_loop(0, WIDE // 384, prob_grad, 0)

        def score_grad(c, carry, g=g):
            cols = ds(c * 128, 128)
            p, dp = pt[g, :, cols].astype(F32), scores[:, cols]
            total = jnp.sum(p * dp, axis=0, keepdims=True)
            dst[:, cols] = (p * (dp - total) * (HEAD_DIM ** -0.5)).astype(BF)
            return carry

        lax.fori_loop(0, WIDE // 128, score_grad, 0, unroll=3)
        pgrad[:, q_at : q_at + GW] = gather_heads(tn(dst[...], packed[:, k_at : k_at + GW])).astype(BF)
        pgrad[:, v_at : v_at + GW] = nn(pt[g], doblk[...]).astype(BF)
        pgrad[:, k_at : k_at + GW] = nn(dst[...], qblk[g]).astype(BF)

    def unproject(n, carry):
        cols = ds(n * 256, 256)
        sg = nt(pgrad[...], wqf[cols, :]).astype(BF).astype(F32)
        tgrad[:, cols] = (gw[:, cols].astype(F32) + sg).astype(BF)
        return carry

    lax.fori_loop(0, D // 256, unproject, 0)
    out_d = halo_out(1, tgrad, land_g, d_out)

    for kind in (0, 1):
        z_copy(kind, 0, 1, z).wait_send()
        x_copy(kind, 0, z, par).wait_send()
        s_copy(kind, 1, 0, z, core).wait_send()

    def sent(d, carry):
        for kind in (0, 1):
            x_copy(kind, d, behind(z, d), par).wait_send()
            s_copy(kind, 0, d, behind(z, d), core).wait_send()
            s_copy(kind, 1, d, behind(z, d), core).wait_send()
        return carry

    lax.fori_loop(1, nz, sent, 0)

    def sent_z(s, carry):
        for kind in (0, 1):
            z_copy(kind, 0, s, behind(z, s - 1)).wait_send()
            z_copy(kind, 1, s - 1, ahead(z, s - 2)).wait_send()
        return carry

    lax.fori_loop(2, ns + 1, sent_z, 0)
    for copy in in_t[0] + in_g[0]:
        copy.wait_send()
    for copies, keep in (out_m, out_d):
        keep.wait()
        for copy in copies:
            copy.wait()


def per_device(n_lat, n_lon, tokens, qkv_weight, out_weight, norm_gain, norm_bias, mixed_grad):
    nz = n_lon // 2
    ns = nz // 2
    hbm = pl.BlockSpec(memory_space=pltpu.HBM)
    cells = (WIN, WIN, LEV, D)
    m_out, d_out = pl.pallas_call(
        functools.partial(kernel, n_lat, n_lon),
        out_shape=[jax.ShapeDtypeStruct(cells, BF)] * 2,
        in_specs=[hbm] * 6,
        out_specs=[pl.BlockSpec(memory_space=pl.ANY)] * 2,
        scratch_shapes=[
            pltpu.VMEM((D, 3 * INNER), BF),
            pltpu.VMEM((INNER, D), BF),
            pltpu.VMEM((1, D), F32),
            pltpu.VMEM((1, D), F32),
            pltpu.VMEM((4, HALF, HALF, LEV, D), BF),
            pltpu.VMEM((4, HALF, HALF, LEV, D), BF),
            pltpu.VMEM((TOK, D), BF),
            pltpu.VMEM((TOK, D), BF),
            pltpu.VMEM((TOK, 3 * INNER), BF),
            pltpu.VMEM((TOK, INNER), BF),
            pltpu.VMEM((TOK, D), BF),
            pltpu.VMEM((TOK, D), BF),
            pltpu.VMEM((TOK, INNER), BF),
            pltpu.VMEM((TOK, 3 * INNER), BF),
            pltpu.VMEM((TOK, WIDE), F32),
            pltpu.VMEM((2, TOK, WIDE), BF),
            pltpu.VMEM((TOK, WIDE), BF),
            pltpu.VMEM((2, WIDE, GW), BF),
            pltpu.VMEM((WIDE, GW), BF),
            pltpu.VMEM((TOK, D), BF),
            pltpu.VMEM((TOK, D), BF),
            pltpu.SemaphoreType.DMA((8,)),
            pltpu.SemaphoreType.DMA((4 * (ns + 1),)),
            pltpu.SemaphoreType.DMA((4 * (ns + 1),)),
            pltpu.SemaphoreType.DMA((2 * nz,)),
            pltpu.SemaphoreType.DMA((2 * nz,)),
            pltpu.SemaphoreType.DMA((4 * nz,)),
            pltpu.SemaphoreType.DMA((4 * nz,)),
            pltpu.SemaphoreType.DMA((16,)),
            pltpu.SemaphoreType.DMA((16,)),
        ],
        compiler_params=pltpu.CompilerParams(
            collective_id=0, has_side_effects=True, vmem_limit_bytes=63 * 1024 * 1024
        ),
    )(
        tokens.transpose(1, 2, 0, 3), mixed_grad.transpose(1, 2, 0, 3), qkv_weight, out_weight,
        norm_gain.reshape(1, D), norm_bias.reshape(1, D),
    )
    return m_out.transpose(2, 0, 1, 3), d_out.transpose(2, 0, 1, 3)


def solution(mesh):
    placed = (
        P(None, "lat", "lon", None),
        P("lon", None),
        P("lon", None),
        P(),
        P(),
        P(None, "lat", "lon", None),
    )
    return jax.shard_map(
        functools.partial(per_device, mesh.shape["lat"], mesh.shape["lon"]),
        mesh=mesh,
        in_specs=placed,
        out_specs=(P(None, "lat", "lon", None), P(None, "lat", "lon", None)),
        check_vma=False,
    )
```

time: 105 us -> 84.4 us (0.80)
  Pallas kernels: 94.4 us -> 79.4 us
  local copies, waits for them, and re-layouts: 7.79 us -> 3.25 us
    pallas_call x1, Pallas kernels: 94.4 us -> 79.4 us  [per_device(): pl.pallas_call(functools.partial(kernel, n_lat, n_lon), out_shape=[jax.Sh...]
    slice x3 -> x0, local copies, waits for them, and re-layouts: 2.07 us -> none  [the longest x2 1.99 us: quarters(): cut[:, i, :, j].reshape(QUARTER, D)]
    unnamed x20 -> x4, local copies, waits for them, and re-layouts: 4.85 us -> 3.25 us
where the time goes in v2:
time: 84.4 us; the launch traced here: 83.3 us
  Pallas kernels  79.4 us (94%)
  local copies, waits for them, and re-layouts  3.25 us (4%)
    pallas_call x1, Pallas kernels, per_device(): pl.pallas_call(functools.partial(kernel, n_lat, n_lon), out_shape=[jax.Sh...  79.4 us
    unnamed x4, local copies, waits for them, and re-layouts  3.25 us

profile of v2, /device:TPU:1, one launch (start us, length us, event | category | flops | bytes accessed | tf_op | source)
XLA Modules:
  0.0 83.3 jit_solution(10224889436562778724)
XLA Ops:
  0.6 79.4 %shard_map.77 = (bf16[12,12,2,1024]{3,2,1,0:T(2,128)(2,1)}, bf16[12,12,2,1024]{3,2,1,0:T(2,128)(2,1)}) custom-call(bf16[12,12,2,1024]{3,2,1,0:T(2,128)(2,1)} %bitcast.6, bf16[12,12,2,1024]{3,2,1,0:T(2,128)(2,1)} %bitcast.7, bf16[32,1536]{1,0:T(8,128)(2,1)} %wq_ref.1, bf16[16,1024]{1,0:T(8,128)(2,1)} %wo_ref.1, f32[1,1024]{1,0:T(1,128)} %bitcast.10, ...), custom_call_target="tpu_custom_call" | custom-call | tf_op jit(solution)/shard_map/pallas_call | solution.py:374
  80.1 0.0 copy-start
  80.1 2.4 %copy.10 = bf16[2,12,12,1024]{3,0,2,1:T(2,128)(2,1)} copy(bf16[2,12,12,1024]{3,0,2,1:T(2,128)(2,1)} %bitcast.9) | data formatting | bytes 1179648
  82.5 0.0 copy-done
  82.5 0.8 copy.11
Async XLA Ops:
  80.1 2.4 %copy-start = (bf16[12,12,2,1024]{3,2,1,0:T(2,128)(2,1)S(1)}, bf16[12,12,2,1024]{3,2,1,0:T(2,128)(2,1)}, u32[]{:S(2)}) copy-start(bf16[12,12,2,1024]{3,2,1,0:T(2,128)(2,1)} %get-tuple-element.5) | copy-start | bytes 1769476

commit v3 on v2

v3 whole, which is shorter than its diff:
```python
import functools

import jax
import jax.numpy as jnp
from jax import lax
from jax.experimental import pallas as pl
from jax.experimental.pallas import tpu as pltpu
from jax.sharding import PartitionSpec as P

MESH = pl.DeviceIdType.MESH
BF = jnp.bfloat16
F32 = jnp.float32

D = 1024
HEADS = 8
HEAD_DIM = 64
LEV = 2
WIN = 12
INNER = 512
HALF = 6
TOK = LEV * WIN * WIN
QUARTER = TOK // 4
GROUP = 4
GW = GROUP * HEAD_DIM
WIDE = GROUP * TOK
ROWS = 32
EPS = 1e-05

HALVES = ((1, 1), (1, 0), (0, 1), (0, 0))


def nt(a, b):
    return lax.dot_general(a, b, (((1,), (1,)), ((), ())), preferred_element_type=F32)


def nn(a, b):
    return lax.dot_general(a, b, (((1,), (0,)), ((), ())), preferred_element_type=F32)


def tn(a, b):
    return lax.dot_general(a, b, (((0,), (0,)), ((), ())), preferred_element_type=F32)


def ds(start, size):
    return pl.ds(pl.multiple_of(start, size), size)


def kernel(
    n_lat, n_lon,
    t_ref, g_ref, wq_ref, wo_ref, gain_hbm, bias_hbm,
    m_out, d_out,
    wqf, wof, gain_ref, bias_ref, land_t, land_g, xw, gw, packed, heads, attn, agrad, hgrad, pgrad,
    scores, pt, dst, qblk, doblk, wide, mixed, tgrad,
    own_sem, zs, zr, ys, yr, xs, xr, ss, sr, hs, hr,
):
    lat, lon = lax.axis_index("lat"), lax.axis_index("lon")
    nz, ny = n_lon // 2, n_lat // 4
    rq, ro = D // n_lon, INNER // n_lon
    core, par, z = lax.rem(lat, 2), lax.rem(lon, 2), lon // 2
    half, y = lat // (2 * ny), lax.rem(lat // 2, ny)
    lat_lo, lat_hi = lax.rem(lat + n_lat - 1, n_lat), lax.rem(lat + 1, n_lat)
    lon_lo, lon_hi = lax.rem(lon + n_lon - 1, n_lon), lax.rem(lon + 1, n_lon)
    sib = (lat + 1 - 2 * core, lon)
    differ = lax.rem(par + core, 2)
    across = lon + 1 - 2 * par
    x_to = (lax.rem(lat + differ * (n_lat // 2), n_lat), across)
    x_from = (lax.rem(lat + (1 - differ) * (n_lat // 2), n_lat), across)
    west, north, diag = (lat, lon_lo), (lat_lo, lon), (lat_lo, lon_lo)
    east, south, far = (lat, lon_hi), (lat_hi, lon), (lat_hi, lon_hi)

    def offset(yy, e):
        far_pair = e // 2
        size = (1 - far_pair) * (yy + 1) + far_pair * (2 * ny - yy)
        return (1 - 2 * lax.rem(e, 2)) * size

    def z_to(e):
        return (lat, 2 * lax.rem(z + offset(y, e) + nz, nz) + par)

    def source(yy, e):
        return lax.rem(z - offset(yy, e) + nz, nz)

    def exists(yy, e):
        return jnp.logical_or(yy > 0, e < 3)

    def y_to(way):
        return ((half * ny + lax.rem(y + 1 - 2 * way + ny, ny)) * 2 + core, lon)

    def line(group, c):
        return lax.rem(y + ny + (0, 2 * c - 1, 1 - 2 * c, 2)[group], ny)

    barrier = pltpu.get_barrier_semaphore()
    met = [z_to(e) for e in range(4)]
    met += [y_to(0), y_to(1), sib, x_to, x_from, west, north, diag, east, south, far]
    for who in met:
        pl.semaphore_signal(barrier, inc=1, device_id=who, device_id_type=MESH)
    pl.semaphore_wait(barrier, len(met))

    def remote(src, dst, send, recv, who):
        return pltpu.make_async_remote_copy(
            src_ref=src, dst_ref=dst, send_sem=send, recv_sem=recv, device_id=who, device_id_type=MESH
        )

    def quarter(ref, k):
        i, j = HALVES[k]
        return ref.at[pl.ds(i * HALF, HALF), pl.ds(j * HALF, HALF)]

    def halo_in(field, src, land):
        copies = [
            remote(quarter(src, k), land.at[k], hs.at[field * 4 + k], hr.at[field * 4 + k], who)
            for k, who in ((1, west), (2, north), (3, diag))
        ]
        return copies, pltpu.make_async_copy(quarter(src, 0), land.at[0], own_sem.at[4 + field])

    in_t = halo_in(0, t_ref, land_t)
    in_g = halo_in(1, g_ref, land_g)
    for copy in in_t[0]:
        copy.start()

    def piece(kind, zq, p, c, both=1):
        if kind == 0:
            return wqf.at[pl.ds(pl.multiple_of((zq * 2 + p) * rq, rq), both * rq), ds(c * 768, 768)]
        return wof.at[pl.ds(pl.multiple_of((zq * 2 + p) * ro, ro), both * ro), ds(c * 512, 512)]

    def own_piece(kind):
        return wq_ref.at[:, ds(core * 768, 768)] if kind == 0 else wo_ref.at[:, ds(core * 512, 512)]

    def z_copy(kind, e, zq):
        i = kind * 4 + e
        return remote(own_piece(kind), piece(kind, zq, par, core), zs.at[i], zr.at[i], z_to(e))

    def y_copy(kind, way, e, zq, to):
        ref, i = piece(kind, zq, par, core), (kind * 3 + way) * 4 + e
        return remote(ref, ref, ys.at[i], yr.at[i], y_to(to))

    def x_copy(kind, slot, zq, p):
        ref, i = piece(kind, zq, p, core), kind * 17 + slot
        return remote(ref, ref, xs.at[i], xr.at[i], x_to)

    def x_own(kind):
        i = kind * 17 + 16
        return remote(own_piece(kind), piece(kind, z, par, core), xs.at[i], xr.at[i], x_to)

    def s_copy(kind, slot, zq, c):
        ref, i = piece(kind, zq, 0, c, 2), kind * 17 + slot
        return remote(ref, ref, ss.at[i], sr.at[i], sib)

    def s_own(kind, c):
        ref, i = piece(kind, z, 1 - par, c), kind * 17 + 16
        return remote(ref, ref, ss.at[i], sr.at[i], sib)

    def each(yy, do):
        def step(e, carry):
            @pl.when(exists(yy, e))
            def _():
                do(e)

            return carry

        lax.fori_loop(0, 4, step, 0)

    def begin(kind):
        each(y, lambda e: z_copy(kind, e, z).start())
        x_own(kind).start()

    def hop_z(kind):
        def do(e):
            zq = source(y, e)
            z_copy(kind, e, zq).wait_recv()
            y_copy(kind, 0, e, zq, 0).start()
            y_copy(kind, 1, e, zq, 1).start()
            x_copy(kind, e, zq, par).start()

        each(y, do)

    def hop_y(kind):
        def near(e):
            zq = source(line(1, core), e)
            y_copy(kind, core, e, zq, core).wait_recv()
            y_copy(kind, 2, e, zq, core).start()
            x_copy(kind, 4 + e, zq, par).start()

        def other(e):
            zq = source(line(2, core), e)
            y_copy(kind, 1 - core, e, zq, core).wait_recv()
            x_copy(kind, 8 + e, zq, par).start()

        each(line(1, core), near)
        each(line(2, core), other)

    def hop_y2(kind):
        def do(e):
            zq = source(line(3, core), e)
            y_copy(kind, 2, e, zq, core).wait_recv()
            x_copy(kind, 12 + e, zq, par).start()

        each(line(3, core), do)

    def hop_x(kind):
        x_copy(kind, 16, z, 1 - par).wait_recv()
        s_own(kind, core).start()
        for group in range(4):
            def do(e, group=group):
                zq = source(line(group, core), e)
                x_copy(kind, group * 4 + e, zq, 1 - par).wait_recv()
                s_copy(kind, group * 4 + e, zq, core).start()

            each(line(group, core), do)

    def finish(kind):
        s_own(kind, 1 - core).wait_recv()
        for group in range(4):
            def do(e, group=group):
                s_copy(kind, group * 4 + e, source(line(group, 1 - core), e), 1 - core).wait_recv()

            each(line(group, 1 - core), do)

    def all_sent(kind):
        x_own(kind).wait_send()
        s_own(kind, core).wait_send()

        def first(e):
            z_copy(kind, e, z).wait_send()
            y_copy(kind, 0, e, source(y, e), 0).wait_send()
            y_copy(kind, 1, e, source(y, e), 1).wait_send()

        each(y, first)
        each(line(1, core), lambda e: y_copy(kind, 2, e, source(line(1, core), e), core).wait_send())
        for group in range(4):
            def do(e, group=group):
                zq = source(line(group, core), e)
                x_copy(kind, group * 4 + e, zq, par).wait_send()
                s_copy(kind, group * 4 + e, zq, core).wait_send()

            each(line(group, core), do)

    local = [
        pltpu.make_async_copy(wq_ref, wqf.at[ds(lon * rq, rq), :], own_sem.at[0]),
        pltpu.make_async_copy(wo_ref, wof.at[ds(lon * ro, ro), :], own_sem.at[1]),
        pltpu.make_async_copy(gain_hbm, gain_ref, own_sem.at[2]),
        pltpu.make_async_copy(bias_hbm, bias_ref, own_sem.at[3]),
        in_t[1],
        in_g[1],
    ]
    begin(0)
    for copy in local:
        copy.start()
    hop_z(0)
    begin(1)
    for copy in in_g[0]:
        copy.start()
    hop_y(0)
    hop_y2(0)

    def rows_of(land, field):
        def step(t, carry):
            k, i = 2 * (t // 3), 2 * lax.rem(t, 3)
            two = [land[k + n, pl.ds(i, 2)].reshape(24, D) for n in (0, 1)]
            field[ds(t * 48, 48), :] = jnp.concatenate(two, axis=0)
            return carry

        lax.fori_loop(0, 6, step, 0)

    for copy in in_t[0]:
        copy.wait_recv()
    for copy in local:
        copy.wait()
    rows_of(land_t, xw)
    hop_x(0)
    hop_z(1)
    finish(0)

    def project(n, carry):
        cols = ds(n * 256, 256)
        packed[:, cols] = nn(xw[...], wqf[:, cols]).astype(BF)
        return carry

    lax.fori_loop(0, 3 * INNER // 256, project, 0)
    hop_y(1)
    hop_y2(1)

    lane_head = lax.broadcasted_iota(jnp.int32, (TOK, GW), 1) // HEAD_DIM
    banned = jnp.where(lat == n_lat - 1, -1e30, 0.0).astype(F32)

    def spread(rows):
        return [rows * (lane_head[0:1] == h).astype(F32).astype(BF) for h in range(GROUP)]

    def gather_heads(wide):
        out = wide[0:TOK, :]
        for h in range(1, GROUP):
            out = jnp.where(lane_head == h, wide[h * TOK : (h + 1) * TOK, :], out)
        return out

    def columns(g):
        return [ds(n * INNER + g * GW, GW) for n in range(3)]

    def narrow(left, right):
        def step(c, carry):
            cols = ds(c * 384, 384)
            wide[cols, :] = tn(left(cols), right)
            return carry

        lax.fori_loop(0, WIDE // 384, step, 0)
        return gather_heads(wide).astype(BF)

    def forward(g, carry):
        q_at, k_at, v_at = columns(g)
        for h, rows in enumerate(spread(packed[:, q_at])):
            qblk[g, h * TOK : (h + 1) * TOK, :] = rows

        def score(c, carry):
            cols = ds(c * 384, 384)
            scores[:, cols] = nt(packed[:, k_at], qblk[g, cols, :])
            return carry

        lax.fori_loop(0, WIDE // 384, score, 0)

        def soften(c, carry):
            cols = ds(c * 128, 128)
            query = lax.rem(c * 128 + lax.broadcasted_iota(jnp.int32, (1, 128), 1), TOK)
            side = (query >= TOK // 2).astype(F32)
            s = jnp.concatenate(
                [scores[: TOK // 2, cols] + side * banned, scores[TOK // 2 :, cols] + (1.0 - side) * banned], axis=0
            )
            top = jnp.max(s, axis=0, keepdims=True)
            e = jnp.exp((s - top) * (HEAD_DIM ** -0.5))
            pt[g, :, cols] = (e * (1.0 / jnp.sum(e, axis=0, keepdims=True))).astype(BF)
            return carry

        lax.fori_loop(0, WIDE // 128, soften, 0, unroll=3)
        heads[:, q_at] = narrow(lambda cols: pt[g, :, cols], packed[:, v_at])

        @pl.when(g == 0)
        def _():
            hop_x(1)

        return carry

    lax.fori_loop(0, HEADS // GROUP, forward, 0)
    finish(1)

    def out_project(n, carry):
        cols = ds(n * 256, 256)
        attn[:, cols] = nn(heads[...], wof[:, cols]).astype(BF)
        return carry

    lax.fori_loop(0, D // 256, out_project, 0)

    for copy in in_g[0]:
        copy.wait_recv()
    rows_of(land_g, gw)

    def norm(c, carry):
        rows = ds(c * ROWS, ROWS)
        a = attn[rows, :].astype(F32)
        gain = gain_ref[...]
        scaled = gw[rows, :].astype(F32) * gain
        centered = a - jnp.mean(a, axis=-1, keepdims=True)
        level = scaled - jnp.mean(scaled, axis=-1, keepdims=True)
        inverse = lax.rsqrt(jnp.mean(centered * centered, axis=-1, keepdims=True) + EPS)
        along = jnp.mean(scaled * centered, axis=-1, keepdims=True) * inverse
        normed = centered * inverse
        mixed[rows, :] = (xw[rows, :].astype(F32) + normed * gain + bias_ref[...]).astype(BF)
        agrad[rows, :] = ((level - normed * along) * inverse).astype(BF)
        return carry

    lax.fori_loop(0, TOK // ROWS, norm, 0, unroll=3)

    def halo_out(field, rows, land, out):
        def step(t, carry):
            k, i = 2 * (t // 3), 2 * lax.rem(t, 3)
            block = rows[ds(t * 48, 48), :]
            for n in (0, 1):
                land[k + n, pl.ds(i, 2)] = block[n * 24 : (n + 1) * 24].reshape(2, HALF, LEV, D)
            return carry

        lax.fori_loop(0, 6, step, 0)
        copies = [
            remote(land.at[k], quarter(out, k), hs.at[(field + 2) * 4 + k], hr.at[(field + 2) * 4 + k], who)
            for k, who in ((1, east), (2, south), (3, far))
        ]
        keep = pltpu.make_async_copy(land.at[0], quarter(out, 0), own_sem.at[6 + field])
        for copy in copies:
            copy.start()
        keep.start()
        return copies, keep

    out_m = halo_out(0, mixed, land_t, m_out)

    def back_project(n, carry):
        cols = ds(n * 256, 256)
        hgrad[:, cols] = nt(agrad[...], wof[cols, :]).astype(BF)
        return carry

    lax.fori_loop(0, INNER // 256, back_project, 0)

    def backward(g, carry):
        q_at, k_at, v_at = columns(g)
        for h, rows in enumerate(spread(hgrad[:, q_at])):
            doblk[h * TOK : (h + 1) * TOK, :] = rows

        def prob_grad(c, carry):
            cols = ds(c * 384, 384)
            scores[:, cols] = nt(packed[:, v_at], doblk[cols, :])
            return carry

        lax.fori_loop(0, WIDE // 384, prob_grad, 0)

        def score_grad(c, carry):
            cols = ds(c * 128, 128)
            p, dp = pt[g, :, cols].astype(F32), scores[:, cols]
            total = jnp.sum(p * dp, axis=0, keepdims=True)
            dst[:, cols] = (p * (dp - total) * (HEAD_DIM ** -0.5)).astype(BF)
            return carry

        lax.fori_loop(0, WIDE // 128, score_grad, 0, unroll=3)
        pgrad[:, q_at] = narrow(lambda cols: dst[:, cols], packed[:, k_at])
        pgrad[:, v_at] = nn(pt[g], doblk[...]).astype(BF)
        pgrad[:, k_at] = nn(dst[...], qblk[g]).astype(BF)
        return carry

    lax.fori_loop(0, HEADS // GROUP, backward, 0)

    def unproject(n, carry):
        cols = ds(n * 256, 256)
        sg = nt(pgrad[...], wqf[cols, :]).astype(BF).astype(F32)
        tgrad[:, cols] = (gw[:, cols].astype(F32) + sg).astype(BF)
        return carry

    lax.fori_loop(0, D // 256, unproject, 0)
    out_d = halo_out(1, tgrad, land_g, d_out)

    for kind in (0, 1):
        all_sent(kind)
    for copy in in_t[0] + in_g[0]:
        copy.wait_send()
    for copies, keep in (out_m, out_d):
        keep.wait()
        for copy in copies:
            copy.wait()


def per_device(n_lat, n_lon, tokens, qkv_weight, out_weight, norm_gain, norm_bias, mixed_grad):
    hbm = pl.BlockSpec(memory_space=pltpu.HBM)
    cells = (WIN, WIN, LEV, D)
    m_out, d_out = pl.pallas_call(
        functools.partial(kernel, n_lat, n_lon),
        out_shape=[jax.ShapeDtypeStruct(cells, BF)] * 2,
        in_specs=[hbm] * 6,
        out_specs=[pl.BlockSpec(memory_space=pl.ANY)] * 2,
        scratch_shapes=[
            pltpu.VMEM((D, 3 * INNER), BF),
            pltpu.VMEM((INNER, D), BF),
            pltpu.VMEM((1, D), F32),
            pltpu.VMEM((1, D), F32),
            pltpu.VMEM((4, HALF, HALF, LEV, D), BF),
            pltpu.VMEM((4, HALF, HALF, LEV, D), BF),
            pltpu.VMEM((TOK, D), BF),
            pltpu.VMEM((TOK, D), BF),
            pltpu.VMEM((TOK, 3 * INNER), BF),
            pltpu.VMEM((TOK, INNER), BF),
            pltpu.VMEM((TOK, D), BF),
            pltpu.VMEM((TOK, D), BF),
            pltpu.VMEM((TOK, INNER), BF),
            pltpu.VMEM((TOK, 3 * INNER), BF),
            pltpu.VMEM((TOK, WIDE), F32),
            pltpu.VMEM((2, TOK, WIDE), BF),
            pltpu.VMEM((TOK, WIDE), BF),
            pltpu.VMEM((2, WIDE, GW), BF),
            pltpu.VMEM((WIDE, GW), BF),
            pltpu.VMEM((WIDE, GW), F32),
            pltpu.VMEM((TOK, D), BF),
            pltpu.VMEM((TOK, D), BF),
            pltpu.SemaphoreType.DMA((8,)),
            pltpu.SemaphoreType.DMA((8,)),
            pltpu.SemaphoreType.DMA((8,)),
            pltpu.SemaphoreType.DMA((24,)),
            pltpu.SemaphoreType.DMA((24,)),
            pltpu.SemaphoreType.DMA((34,)),
            pltpu.SemaphoreType.DMA((34,)),
            pltpu.SemaphoreType.DMA((34,)),
            pltpu.SemaphoreType.DMA((34,)),
            pltpu.SemaphoreType.DMA((16,)),
            pltpu.SemaphoreType.DMA((16,)),
        ],
        compiler_params=pltpu.CompilerParams(
            collective_id=0, has_side_effects=True, vmem_limit_bytes=63 * 1024 * 1024
        ),
    )(
        tokens.transpose(1, 2, 0, 3), mixed_grad.transpose(1, 2, 0, 3), qkv_weight, out_weight,
        norm_gain.reshape(1, D), norm_bias.reshape(1, D),
    )
    return m_out.transpose(2, 0, 1, 3), d_out.transpose(2, 0, 1, 3)


def solution(mesh):
    placed = (
        P(None, "lat", "lon", None),
        P("lon", None),
        P("lon", None),
        P(),
        P(),
        P(None, "lat", "lon", None),
    )
    return jax.shard_map(
        functools.partial(per_device, mesh.shape["lat"], mesh.shape["lon"]),
        mesh=mesh,
        in_specs=placed,
        out_specs=(P(None, "lat", "lon", None), P(None, "lat", "lon", None)),
        check_vma=False,
    )
```

time: 84.4 us -> 85 us (level); the launches traced: 83.3 us -> 84.8 us
  Pallas kernels: 79.4 us -> 80.9 us
    pallas_call x1, Pallas kernels: 79.4 us -> 80.9 us  [per_device(): pl.pallas_call(functools.partial(kernel, n_lat, n_lon), out_shape=[jax.Sh...]
where the time goes in v3:
time: 85 us; the launch traced here: 84.8 us
  Pallas kernels  80.9 us (95%)
  local copies, waits for them, and re-layouts  3.25 us (4%)
    pallas_call x1, Pallas kernels, per_device(): pl.pallas_call(functools.partial(kernel, n_lat, n_lon), out_shape=[jax.Sh...  80.9 us
    unnamed x4, local copies, waits for them, and re-layouts  3.25 us

profile of v3, /device:TPU:1, one launch (start us, length us, event | category | flops | bytes accessed | tf_op | source)
XLA Modules:
  0.0 84.8 jit_solution(17161093700129406314)
XLA Ops:
  0.6 80.9 %shard_map.77 = (bf16[12,12,2,1024]{3,2,1,0:T(2,128)(2,1)}, bf16[12,12,2,1024]{3,2,1,0:T(2,128)(2,1)}) custom-call(bf16[12,12,2,1024]{3,2,1,0:T(2,128)(2,1)} %bitcast.6, bf16[12,12,2,1024]{3,2,1,0:T(2,128)(2,1)} %bitcast.7, bf16[32,1536]{1,0:T(8,128)(2,1)} %wq_ref.1, bf16[16,1024]{1,0:T(8,128)(2,1)} %wo_ref.1, f32[1,1024]{1,0:T(1,128)} %bitcast.10, ...), custom_call_target="tpu_custom_call" | custom-call | tf_op jit(solution)/shard_map/pallas_call | solution.py:445
  81.6 0.0 copy-start
  81.6 2.4 %copy.10 = bf16[2,12,12,1024]{3,0,2,1:T(2,128)(2,1)} copy(bf16[2,12,12,1024]{3,0,2,1:T(2,128)(2,1)} %bitcast.9) | data formatting | bytes 1179648
  84.0 0.0 copy-done
  84.0 0.8 copy.11
Async XLA Ops:
  81.6 2.4 %copy-start = (bf16[12,12,2,1024]{3,2,1,0:T(2,128)(2,1)S(1)}, bf16[12,12,2,1024]{3,2,1,0:T(2,128)(2,1)}, u32[]{:S(2)}) copy-start(bf16[12,12,2,1024]{3,2,1,0:T(2,128)(2,1)} %get-tuple-element.5) | copy-start | bytes 1769476
